TPU v7x, 32 devices: a whole 2x2x4 slice. The times are simulated.
32 devices in a mesh: row: 4 (over x, core), col: 8 (over z, y).
Axes of the slice: x: 2, y: 2, z: 4, core: 2. Of those that a mesh axis runs over, the one named last changes fastest.
Arguments:
- right_sides: bfloat16 [16384, 6144], P('row', 'col'), may hold values from -6 to 6
- factor_panels: bfloat16 [16384, 1024], P(('row', 'col')), may hold values from -0.1875 to 0.1875
- inverse_blocks: float32 [4, 256, 256], replicated, may hold values from -1 to 1, as said below
Outputs:
- solved_sides: float32 [16384, 6144], P('row', 'col')
Inputs may be any that keep to these rules, and one draw needn't show every extreme that they name: `inverse_blocks`: each block is unit lower triangular.
All inputs are finite; a program needn't handle non-finite values.
Results may differ from a plain program's by a relative error of at most 0.003.
Values may be sent and summed in bfloat16 or wider, within the bound.
A program may use at most 192 MiB of HBM per device.

v0:
```python
import jax
import jax.numpy as jnp
from jax import lax
from jax.sharding import PartitionSpec as P


def from_root(value, axis, root):
    mine = lax.axis_index(axis) == root
    return lax.psum(jnp.where(mine, value, jnp.zeros_like(value)), axis)


def publish(solved, panel_num):
    return from_root(solved.astype(jnp.bfloat16), "row", panel_num)


def per_device(right_sides, factor_panels, inverse_blocks):
    panel_count = inverse_blocks.shape[0]
    panel_width = inverse_blocks.shape[1]
    row_index = lax.axis_index("row")
    current = right_sides.astype(jnp.float32)
    for panel_num in range(panel_count):
        leading = current[:panel_width]
        solved = jnp.dot(inverse_blocks[panel_num], leading, precision=lax.Precision.HIGHEST)
        shared = publish(solved, panel_num)
        columns = factor_panels[:, panel_num * panel_width : (panel_num + 1) * panel_width]
        update = jnp.dot(
            lax.all_gather(columns, "col", axis=0, tiled=True),
            shared,
            preferred_element_type=jnp.float32,
        )
        updated_first = jnp.where(row_index > panel_num, leading - update[:panel_width], leading)
        new_first = jnp.where(row_index == panel_num, solved, updated_first)
        current = jnp.concatenate([new_first, current[panel_width:] - update[panel_width:]], 0)
    return current


def solution(mesh):
    placed = (P("row", "col"), P(("row", "col"), None), P())
    return jax.shard_map(
        per_device, mesh=mesh, in_specs=placed, out_specs=P("row", "col"), check_vma=False
    )
```

profile of v0, /device:TPU:0, one launch (start us, length us, event | category | flops | bytes accessed | tf_op | source)
XLA Modules:
  0.0 264.0 jit_solution(13297560844712373202)
XLA Ops:
  7.4 0.0 all-reduce.5.cloned.1.call-start
  7.4 2.3 convert_select_fusion.3
  9.7 0.0 all-reduce.5.cloned.1.call-update
  9.7 0.0 all-gather.5.cloned.1.call-start
  9.8 2.2 fusion.14
  12.0 0.0 all-gather.5.cloned.1.call-update
  12.0 0.0 all-gather.7.cloned.1.call-start
  12.1 0.5 all-gather.7.cloned.1.call-update
  12.6 0.0 all-reduce.7.cloned.1.call-start
  12.7 8.6 %convert_element_type.15 = f32[4096,768]{1,0:T(8,128)} convert(bf16[4096,768]{1,0:T(8,128)(2,1)} %param.3) | non-fusion elementwise | flops 3145728 | bytes 18874368 | tf_op jit(solution)/shard_map/convert_element_type | solution.py:20
  21.2 0.0 copy-start.3
  21.2 24.7 %all-reduce.5.cloned.1.call-done = bf16[256,768]{1,0:T(8,128)(2,1)} async-done(((bf16[256,768]{1,0:T(8,128)(2,1)}), bf16[256,768]{1,0:T(8,128)(2,1)}) %all-reduce.5.cloned.1.call-update) | async-done | bytes 393232 | tf_op jit(solution)/shard_map/psum | solution.py:9
  45.9 18.3 %all-gather.5.cloned.1.call-done = bf16[4096,256]{1,0:T(8,128)(2,1)} async-done(((bf16[512,256]{1,0:T(8,128)(2,1)}), bf16[4096,256]{1,0:T(8,128)(2,1)}) %all-gather.5.cloned.1.call-update) | async-done | bytes 2097168 | tf_op jit(solution)/shard_map/all_gather | solution.py:27
  64.2 3.4 %convolution_bitcast_fusion.3 = f32[4096,768]{1,0:T(8,128)S(1)} fusion(bf16[4096,256]{1,0:T(8,128)(2,1)} %all-gather.5.cloned.1.call-done, bf16[256,768]{1,0:T(8,128)(2,1)} %all-reduce.5.cloned.1.call-done), kind=kOutput, calls=%fused_computation.8 | convolution fusion | flops 1610612736 | bytes 15073280 | tf_op jit(solution)/shard_map/dot_general | solution.py:26
  67.6 0.0 copy-start
  67.7 4.5 %copy-done = f32[4096,768]{1,0:T(8,128)} copy-done((f32[4096,768]{1,0:T(8,128)}, f32[4096,768]{1,0:T(8,128)S(1)}, u32[]{:S(2)}) %copy-start) | copy-done | bytes 12582936
  72.2 1.3 fusion
  73.5 0.0 copy-done.3
  73.5 1.6 convert_select_fusion.2
  75.1 0.0 all-reduce.7.cloned.1.call-update
  75.2 0.0 all-gather.9.cloned.1.call-start
  75.2 0.5 all-gather.9.cloned.1.call-update
  75.7 0.0 all-reduce.9.cloned.1.call-start
  75.8 38.2 %all-gather.7.cloned.1.call-done = bf16[4096,256]{1,0:T(8,128)(2,1)} async-done(((bf16[512,256]{1,0:T(8,128)(2,1)}), bf16[4096,256]{1,0:T(8,128)(2,1)}) %all-gather.7.cloned.1.call-update) | async-done | bytes 2097168 | tf_op jit(solution)/shard_map/all_gather | solution.py:27
  114.0 0.0 all-reduce.7.cloned.1.call-done
  114.0 3.4 %convolution_bitcast_fusion.2 = f32[4096,768]{1,0:T(8,128)S(1)} fusion(bf16[4096,256]{1,0:T(8,128)(2,1)} %all-gather.7.cloned.1.call-done, bf16[256,768]{1,0:T(8,128)(2,1)} %all-reduce.7.cloned.1.call-done), kind=kOutput, calls=%fused_computation.7 | convolution fusion | flops 1610612736 | bytes 15073280 | tf_op jit(solution)/shard_map/dot_general | solution.py:26
  117.4 0.0 copy-start.1
  117.4 4.5 %copy-done.1 = f32[4096,768]{1,0:T(8,128)} copy-done((f32[4096,768]{1,0:T(8,128)}, f32[4096,768]{1,0:T(8,128)S(1)}, u32[]{:S(2)}) %copy-start.1) | copy-done | bytes 12582936
  121.9 0.1 fusion.1
  122.0 1.6 convert_select_fusion.1
  123.6 0.0 all-reduce.9.cloned.1.call-update
  123.7 0.0 all-gather.11.cloned.1.call-start
  123.7 0.7 all-gather.11.cloned.1.call-update
  124.4 0.2 all-reduce.11.cloned.1.call-start
  124.6 39.0 %all-gather.9.cloned.1.call-done = bf16[4096,256]{1,0:T(8,128)(2,1)} async-done(((bf16[512,256]{1,0:T(8,128)(2,1)}), bf16[4096,256]{1,0:T(8,128)(2,1)}) %all-gather.9.cloned.1.call-update) | async-done | bytes 2097168 | tf_op jit(solution)/shard_map/all_gather | solution.py:27
  163.7 0.0 all-reduce.9.cloned.1.call-done
  163.7 3.4 %convolution_bitcast_fusion.1 = f32[4096,768]{1,0:T(8,128)S(1)} fusion(bf16[4096,256]{1,0:T(8,128)(2,1)} %all-gather.9.cloned.1.call-done, bf16[256,768]{1,0:T(8,128)(2,1)} %all-reduce.9.cloned.1.call-done), kind=kOutput, calls=%fused_computation.6 | convolution fusion | flops 1610612736 | bytes 15073280 | tf_op jit(solution)/shard_map/dot_general | solution.py:26
  167.1 0.0 copy-start.2
  167.1 4.6 %copy-done.2 = f32[4096,768]{1,0:T(8,128)} copy-done((f32[4096,768]{1,0:T(8,128)}, f32[4096,768]{1,0:T(8,128)S(1)}, u32[]{:S(2)}) %copy-start.2) | copy-done | bytes 12582936
  171.7 0.1 fusion.2
  171.9 1.6 convert_select_fusion
  173.5 0.0 all-reduce.11.cloned.1.call-update
  173.5 40.1 %all-gather.11.cloned.1.call-done = bf16[4096,256]{1,0:T(8,128)(2,1)} async-done(((bf16[512,256]{1,0:T(8,128)(2,1)}), bf16[4096,256]{1,0:T(8,128)(2,1)}) %all-gather.11.cloned.1.call-update) | async-done | bytes 2097168 | tf_op jit(solution)/shard_map/all_gather | solution.py:27
  213.6 0.0 all-reduce.11.cloned.1.call-done
  213.6 7.9 %convolution_bitcast_fusion = f32[4096,768]{1,0:T(8,128)} fusion(bf16[4096,256]{1,0:T(8,128)(2,1)} %all-gather.11.cloned.1.call-done, bf16[256,768]{1,0:T(8,128)(2,1)} %all-reduce.11.cloned.1.call-done), kind=kOutput, calls=%fused_computation.5 | convolution fusion | flops 1610612736 | bytes 15073280 | tf_op jit(solution)/shard_map/dot_general | solution.py:26
  221.5 24.0 %slice_subtract_fusion = f32[3840,768]{1,0:T(8,128)} fusion(f32[4096,768]{1,0:T(8,128)} %convolution_bitcast_fusion, f32[4096,768]{1,0:T(8,128)} %copy-done.2, f32[4096,768]{1,0:T(8,128)} %copy-done.1, f32[4096,768]{1,0:T(8,128)} %copy-done, f32[4096,768]{1,0:T(8,128)} %convert_element_type.15), kind=kLoop, calls=%fused_computation.1 | loop fusion | flops 11796480 | bytes 70778880 | tf_op jit(solution)/shard_map/sub | solution.py:33
  245.5 1.3 fusion.3
  246.7 9.9 %pad_maximum_fusion = f32[4096,768]{1,0:T(8,128)} fusion(f32[3840,768]{1,0:T(8,128)} %slice_subtract_fusion, f32[256,768]{1,0:T(8,128)S(1)} %fusion.3), kind=kLoop, calls=%fused_computation | loop fusion | flops 3145728 | bytes 25165824 | tf_op jit(solution)/shard_map/concatenate | solution.py:33
Async XLA Ops:
  7.4 38.6 %all-reduce.5.cloned.1.call-start = ((), (), s32[]{:S(2)}) async-start(), calls=%async_computation | async-start | bytes 786432 | tf_op jit(solution)/shard_map/psum | solution.py:9
  9.7 54.5 %all-gather.5.cloned.1.call-start = ((), (), s32[]{:S(2)}) async-start(), calls=%async_computation.1 | async-start | bytes 2359296 | tf_op jit(solution)/shard_map/all_gather | solution.py:27
  12.0 101.9 %all-gather.7.cloned.1.call-start = ((), (), s32[]{:S(2)}) async-start(), calls=%async_computation.3 | async-start | bytes 2359296 | tf_op jit(solution)/shard_map/all_gather | solution.py:27
  12.6 101.3 %all-reduce.7.cloned.1.call-start = ((), (), s32[]{:S(2)}) async-start(), calls=%async_computation.2 | async-start | bytes 786432 | tf_op jit(solution)/shard_map/psum | solution.py:9
  21.2 52.3 %copy-start.3 = (f32[4,256,256]{2,1,0:T(8,128)S(1)}, f32[4,256,256]{2,1,0:T(8,128)}, u32[]{:S(2)}) copy-start(f32[4,256,256]{2,1,0:T(8,128)} %param.5) | copy-start | bytes 3145732
  67.6 4.5 %copy-start = (f32[4096,768]{1,0:T(8,128)}, f32[4096,768]{1,0:T(8,128)S(1)}, u32[]{:S(2)}) copy-start(f32[4096,768]{1,0:T(8,128)S(1)} %convolution_bitcast_fusion.3) | copy-start | bytes 37748740
  75.2 88.5 %all-gather.9.cloned.1.call-start = ((), (), s32[]{:S(2)}) async-start(), calls=%async_computation.5 | async-start | bytes 2359296 | tf_op jit(solution)/shard_map/all_gather | solution.py:27
  75.7 88.0 %all-reduce.9.cloned.1.call-start = ((), (), s32[]{:S(2)}) async-start(), calls=%async_computation.4 | async-start | bytes 786432 | tf_op jit(solution)/shard_map/psum | solution.py:9
  117.4 4.5 %copy-start.1 = (f32[4096,768]{1,0:T(8,128)}, f32[4096,768]{1,0:T(8,128)S(1)}, u32[]{:S(2)}) copy-start(f32[4096,768]{1,0:T(8,128)S(1)} %convolution_bitcast_fusion.2) | copy-start | bytes 37748740
  123.7 89.9 %all-gather.11.cloned.1.call-start = ((), (), s32[]{:S(2)}) async-start(), calls=%async_computation.7 | async-start | bytes 2359296 | tf_op jit(solution)/shard_map/all_gather | solution.py:27
  124.4 89.2 %all-reduce.11.cloned.1.call-start = ((), (), s32[]{:S(2)}) async-start(), calls=%async_computation.6 | async-start | bytes 786432 | tf_op jit(solution)/shard_map/psum | solution.py:9
  167.1 4.6 %copy-start.2 = (f32[4096,768]{1,0:T(8,128)}, f32[4096,768]{1,0:T(8,128)S(1)}, u32[]{:S(2)}) copy-start(f32[4096,768]{1,0:T(8,128)S(1)} %convolution_bitcast_fusion.1) | copy-start | bytes 37748740
Sparse Core Ops, SparseCore 0:
  10.5 35.3 all-reduce.4
  75.3 31.1 all-reduce.6
  123.8 31.1 all-reduce.8
  173.6 31.1 all-reduce.10
Sparse Core Ops, SparseCore 1:
  12.3 51.9 all-gather.4
  66.2 47.7 all-gather.6
  116.0 47.7 all-gather.8
  165.8 47.7 all-gather.10
where the time goes:
time: 264 us
  waiting for transfers between devices  162 us (61%)
  other arithmetic  45.3 us (17%)
  matrix products  25.3 us (10%)
  local copies, waits for them, and re-layouts  15.9 us (6%)
  between operations  14.9 us (6%)
    all_gather x4, waiting for transfers between devices, per_device(): lax.all_gather(columns, 'col', axis=0, tiled=True)  136 us
    psum x4, waiting for transfers between devices, from_root(): return lax.psum(jnp.where(mine, value, jnp.zeros_like(value)), axis)  24.7 us
    sub x1, other arithmetic, per_device(): current[panel_width:] - update[panel_width:]  24 us
    dot_general x4, matrix products, per_device(): jnp.dot(lax.all_gather(columns, 'col', axis=0, tiled=True), shared, prefe...  18.2 us
    unnamed x8, local copies, waits for them, and re-layouts  13.6 us
    concatenate x1, other arithmetic, per_device(): jnp.concatenate([new_first, current[panel_width:] - update[panel_width:]]...  9.94 us
    convert_element_type x1, other arithmetic, per_device(): current = right_sides.astype(jnp.float32)  8.55 us
    dot_general x4, matrix products, per_device(): jnp.dot(inverse_blocks[panel_num], leading, precision=lax.Precision.HIGHEST)  7.16 us
  transfers between devices with their start and end apart: 8, of which 5 were waited for; matrix products, arithmetic and copies ran while one was open for 10% of the time, Pallas kernels for 0%

commit v1 on v0

v1 whole, which is shorter than its diff:
```python
import functools

import jax
import jax.numpy as jnp
from jax import lax
from jax.experimental import pallas as pl
from jax.experimental.pallas import tpu as pltpu
from jax.sharding import PartitionSpec as P

MESH = pl.DeviceIdType.MESH
UP, DOWN, RIGHT, LEFT = range(4)


def every(*conditions):
    kept = [c for c in conditions if c is not True]
    if not kept:
        return True
    return functools.reduce(jnp.logical_and, kept)


def run_if(condition, action):
    if condition is True:
        action()
    else:
        pl.when(condition)(action)


def gather_and_solve(
    rows, layers, lanes, parts,
    rhs_ref, factor_ref, inverse_ref,
    gathered, shared, own_solved,
    lead, panel_rows,
    send_sem, recv_sem, lead_send, lead_recv, panel_send, panel_recv, local_sem,
):
    panels, width, _ = inverse_ref.shape
    depth = factor_ref.shape[0]
    piece = depth // parts
    row = lax.axis_index("row")
    col = lax.axis_index("col")
    z, y = col // lanes, col % lanes
    balanced = lanes == 2 and layers % 2 == 0 and parts % 2 == 0 and width * 2 <= depth
    half = parts // 2
    panel_parts = width // piece

    barrier = pltpu.get_barrier_semaphore()
    can = {UP: z + 1 < layers, DOWN: z >= 1, RIGHT: y + 1 < lanes, LEFT: y >= 1}
    shift = {UP: lanes, DOWN: -lanes, RIGHT: 1, LEFT: -1}
    for way in (UP, DOWN, RIGHT, LEFT):
        def greet(way=way):
            pl.semaphore_signal(barrier, inc=1, device_id=(row, col + shift[way]), device_id_type=MESH)
        run_if(can[way], greet)
    for off in range(1, rows):
        pl.semaphore_signal(barrier, inc=1, device_id=(lax.rem(row + off, rows), col), device_id_type=MESH)
    neighbours = sum(jnp.where(can[way], 1, 0) for way in (UP, DOWN, RIGHT, LEFT))
    pl.semaphore_wait(barrier, rows - 1 + neighbours)

    pending = []

    def place(source, q):
        return gathered.at[pl.ds(pl.multiple_of(source * depth + q * piece, piece), piece)]

    def copy_of(way, target, source, q, own):
        src = factor_ref.at[pl.ds(q * piece, piece)] if own else place(source, q)
        return pltpu.make_async_remote_copy(
            src_ref=src, dst_ref=place(source, q),
            send_sem=send_sem.at[way, source, q], recv_sem=recv_sem.at[source, q],
            device_id=(row, target), device_id_type=MESH,
        )

    def send(condition, way, target, source, q, own=False):
        run_if(condition, lambda: copy_of(way, target, source, q, own).start())
        pending.append((condition, lambda: copy_of(way, target, source, q, own).wait_send()))

    def arrive(condition, source, q):
        run_if(condition, lambda: copy_of(UP, col, source, q, False).wait_recv())

    def send_own(q):
        for way in (UP, DOWN, RIGHT, LEFT):
            send(can[way], way, col + shift[way], col, q, own=True)

    def send_lead(off):
        target = lax.rem(row + off, rows)
        return pltpu.make_async_remote_copy(
            src_ref=rhs_ref.at[pl.ds(0, width)], dst_ref=lead.at[row],
            send_sem=lead_send.at[off], recv_sem=lead_recv.at[row],
            device_id=(target, col), device_id_type=MESH,
        )

    def send_panel(k, off, q):
        target = lax.rem(row + off, rows)
        span = (pl.ds(q * piece, piece), pl.ds(0, k * width))
        return pltpu.make_async_remote_copy(
            src_ref=gathered.at[span], dst_ref=panel_rows.at[(k - 1,) + span],
            send_sem=panel_send.at[off, q], recv_sem=panel_recv.at[k - 1, q],
            device_id=(target, col), device_id_type=MESH,
        )

    send_own(0)
    send_own(1)
    owner = row < panels
    own_block = pltpu.make_async_copy(factor_ref, gathered.at[pl.ds(pl.multiple_of(col * depth, depth), depth)], local_sem.at[0])
    own_block.start()
    for off in range(1, rows):
        run_if(owner, lambda off=off: send_lead(off).start())
        pending.append((owner, lambda off=off: send_lead(off).wait_send()))
    own_lead = pltpu.make_async_copy(rhs_ref.at[pl.ds(0, width)], lead.at[lax.rem(row, panels)], local_sem.at[1])
    run_if(owner, own_lead.start)
    run_if(owner, own_lead.wait)
    own_block.wait()

    def exchange_panel(q):
        for k in range(1, panels):
            for off in range(1, rows):
                run_if(row == k, lambda k=k, off=off: send_panel(k, off, q).start())
                pending.append((row == k, lambda k=k, off=off: send_panel(k, off, q).wait_send()))

    def pass_on(q):
        for d in range(1, layers):
            below, above = z >= d, z + d < layers
            source = col - d * lanes
            arrive(below, source, q)
            send(every(below, can[UP]), UP, col + lanes, source, q)
            kept = z % 2 == 0 if balanced and d == 1 and q >= half else True
            for way in (RIGHT, LEFT):
                send(every(below, can[way], kept), way, col + shift[way], source, q)
            source_above = col + d * lanes
            arrive(above, source_above, q)
            send(every(above, can[DOWN]), DOWN, col - lanes, source_above, q)
            kept = z % 2 == 1 if balanced and d == 1 and q >= half else True
            for way in (RIGHT, LEFT):
                send(every(above, can[way], kept), way, col + shift[way], source_above, q)

    other = z * lanes + (lanes - 1 - y)
    for q in range(parts):
        if q + 2 < parts:
            send_own(q + 2)
        pass_on(q)
        if balanced:
            if 1 <= q <= panel_parts:
                arrive(y == 1, 0, q - 1)
                exchange_panel(q - 1)
            if q >= half:
                arrive(True, other, q)
                send(True, z % 2, col + lanes * (1 - 2 * (z % 2)), other, q)
    if not balanced:
        for q in range(parts):
            for s in range(1, lanes):
                for layer in range(layers):
                    from_left, from_right = y >= s, y + s < lanes
                    arrive(from_left, layer * lanes + y - s, q)
                    send(every(from_left, can[RIGHT]), RIGHT, col + 1, layer * lanes + y - s, q)
                    arrive(from_right, layer * lanes + y + s, q)
                    send(every(from_right, can[LEFT]), LEFT, col - 1, layer * lanes + y + s, q)
        for q in range(panel_parts):
            exchange_panel(q)

    for k in range(1, panels):
        def own_rows(k=k):
            span = (pl.ds(0, width), pl.ds(0, k * width))
            move = pltpu.make_async_copy(gathered.at[span], panel_rows.at[(k - 1,) + span], local_sem.at[2])
            move.start()
            move.wait()
        def other_rows(k=k):
            for q in range(panel_parts):
                send_panel(k, 1, q).wait_recv()
        run_if(row == k, own_rows)
        run_if(row != k, other_rows)
    for k in range(panels):
        def other_lead(k=k):
            pltpu.make_async_remote_copy(
                src_ref=lead.at[k], dst_ref=lead.at[k], send_sem=lead_send.at[0], recv_sem=lead_recv.at[k],
                device_id=(row, col), device_id_type=MESH,
            ).wait_recv()
        run_if(row != k, other_lead)

    tile = min(256, shared.shape[1])

    @pl.loop(0, shared.shape[1] // tile)
    def _(step):
        at = pl.ds(pl.multiple_of(step * tile, tile), tile)
        for k in range(panels):
            current = lead[k, :, at].astype(jnp.float32)
            if k:
                current = current - jnp.dot(
                    panel_rows[k - 1, :, : k * width], shared[: k * width, at], preferred_element_type=jnp.float32
                )
            solved = jnp.dot(
                inverse_ref[k], current, precision=lax.Precision.HIGHEST, preferred_element_type=jnp.float32
            )
            shared[k * width : (k + 1) * width, at] = solved.astype(jnp.bfloat16)

            def keep(solved=solved):
                own_solved[:, at] = solved
            run_if(row == k, keep)

    if balanced:
        for layer in range(layers):
            for q in range(parts):
                source = layer * lanes + (lanes - 1 - y)
                if layer == 0 and q < panel_parts:
                    arrive(y == 0, source, q)
                elif q >= half:
                    arrive(z != layer, source, q)
                else:
                    arrive(True, source, q)
    for condition, finish in pending:
        run_if(condition, finish)


def multiply(row_ref, rhs_ref, gathered_ref, shared_ref, solved_ref, out_ref):
    step = pl.program_id(0)
    width = solved_ref.shape[0]
    update = jnp.dot(gathered_ref[...], shared_ref[...], preferred_element_type=jnp.float32)
    out_ref[...] = rhs_ref[...].astype(jnp.float32) - update

    @pl.when(jnp.logical_and(step == 0, row_ref[0] == 1))
    def _():
        out_ref[:width] = solved_ref[...]


def per_device(rows, layers, lanes, right_sides, factor_panels, inverse_blocks):
    height, count = right_sides.shape
    panels, width, _ = inverse_blocks.shape
    depth, across = factor_panels.shape
    cols = layers * lanes
    parts = 4
    dma = pltpu.SemaphoreType.DMA
    anywhere = pl.BlockSpec(memory_space=pl.ANY)
    in_vmem = pl.BlockSpec(memory_space=pltpu.VMEM)
    gathered, shared, own_solved = pl.pallas_call(
        functools.partial(gather_and_solve, rows, layers, lanes, parts),
        out_shape=(
            jax.ShapeDtypeStruct((cols * depth, across), factor_panels.dtype),
            jax.ShapeDtypeStruct((panels * width, count), jnp.bfloat16),
            jax.ShapeDtypeStruct((width, count), jnp.float32),
        ),
        in_specs=[anywhere, anywhere, in_vmem],
        out_specs=(anywhere, in_vmem, in_vmem),
        scratch_shapes=[
            pltpu.VMEM((panels, width, count), right_sides.dtype),
            pltpu.VMEM((panels - 1, width, (panels - 1) * width), factor_panels.dtype),
            dma((4, cols, parts)), dma((cols, parts)),
            dma((rows,)), dma((panels,)), dma((rows, parts)), dma((panels, parts)), dma((3,)),
        ],
        compiler_params=pltpu.CompilerParams(
            collective_id=0, has_side_effects=True, vmem_limit_bytes=24 << 20
        ),
    )(right_sides, factor_panels, inverse_blocks)

    tile = 512
    is_owner = (lax.axis_index("row") < panels).astype(jnp.int32).reshape(1)
    return pl.pallas_call(
        multiply,
        out_shape=jax.ShapeDtypeStruct((height, count), jnp.float32),
        grid_spec=pltpu.PrefetchScalarGridSpec(
            num_scalar_prefetch=1,
            grid=(height // tile,),
            in_specs=[
                pl.BlockSpec((tile, count), lambda i, s: (i, 0)),
                pl.BlockSpec((tile, across), lambda i, s: (i, 0)),
                pl.BlockSpec((across, count), lambda i, s: (0, 0)),
                pl.BlockSpec((width, count), lambda i, s: (0, 0)),
            ],
            out_specs=pl.BlockSpec((tile, count), lambda i, s: (i, 0)),
        ),
        compiler_params=pltpu.CompilerParams(vmem_limit_bytes=32 << 20),
    )(is_owner, right_sides, gathered, shared, own_solved)


def solution(mesh):
    rows, cols = mesh.shape["row"], mesh.shape["col"]
    lanes = max(1, rows // 2)
    placed = (P("row", "col"), P(("row", "col"), None), P())
    return jax.shard_map(
        functools.partial(per_device, rows, cols // lanes, lanes),
        mesh=mesh, in_specs=placed, out_specs=P("row", "col"), check_vma=False,
    )
```

time: 264 us -> 107 us (0.41)
  waiting for transfers between devices: 162 us -> 0 us
  Pallas kernels: 0 us -> 102 us
  other arithmetic: 45.3 us -> 0 us
  matrix products: 25.3 us -> 0 us
  between operations: 14.9 us -> 0.02 us
  local copies, waits for them, and re-layouts: 15.9 us -> 5.24 us
    all_gather x4 -> x0, waiting for transfers between devices: 136 us -> none  [per_device(): lax.all_gather(columns, 'col', axis=0, tiled=True)]
    pallas_call x0 -> x2, Pallas kernels: none -> 102 us  [the longest x1 92.3 us: per_device(): pl.pallas_call(functools.partial(gather_and_solve, rows, layers, lanes, p...]
    dot_general x8 -> x0, matrix products: 25.3 us -> none  [the longest x4 18.2 us: per_device(): jnp.dot(lax.all_gather(columns, 'col', axis=0, tiled=True), shared, prefe...]
    psum x4 -> x0, waiting for transfers between devices: 24.7 us -> none  [from_root(): return lax.psum(jnp.where(mine, value, jnp.zeros_like(value)), axis)]
    sub x1 -> x0, other arithmetic: 24 us -> none  [per_device(): current[panel_width:] - update[panel_width:]]
    concatenate x1 -> x0, other arithmetic: 9.94 us -> none  [per_device(): jnp.concatenate([new_first, current[panel_width:] - update[panel_width:]]...]
    convert_element_type x1 -> x0, other arithmetic: 8.55 us -> none  [per_device(): current = right_sides.astype(jnp.float32)]
    unnamed x8, local copies, waits for them, and re-layouts: 13.6 us -> 5.24 us
  transfers between devices with their start and end apart: 8 -> 0, of which waited for: 5 -> 0; matrix products, arithmetic and copies ran while one was open for 10% -> 0% of each run, Pallas kernels for 0% -> 0%
where the time goes in v1:
time: 107 us
  Pallas kernels  102 us (95%)
  local copies, waits for them, and re-layouts  5.24 us (5%)
    pallas_call x1, Pallas kernels, per_device(): pl.pallas_call(functools.partial(gather_and_solve, rows, layers, lanes, p...  92.3 us
    pallas_call x1, Pallas kernels, per_device(): pl.pallas_call(multiply, out_shape=jax.ShapeDtypeStruct((height, count),...  9.58 us
    unnamed x8, local copies, waits for them, and re-layouts  5.24 us

profile of v1, /device:TPU:0, one launch (start us, length us, event | category | flops | bytes accessed | tf_op | source)
XLA Modules:
  0.0 107.2 jit_solution(14871676941179005381)
XLA Ops:
  0.0 0.0 copy-start
  0.0 2.8 %copy-done = bf16[4096,768]{1,0:T(8,128)(2,1)S(1)} copy-done((bf16[4096,768]{1,0:T(8,128)(2,1)S(1)}, bf16[4096,768]{1,0:T(8,128)(2,1)}, u32[]{:S(2)}) %copy-start) | copy-done | bytes 6291480
  2.8 0.0 copy-start.2
  2.8 1.2 %copy-done.2 = bf16[512,1024]{1,0:T(8,128)(2,1)S(1)} copy-done((bf16[512,1024]{1,0:T(8,128)(2,1)S(1)}, bf16[512,1024]{1,0:T(8,128)(2,1)}, u32[]{:S(2)}) %copy-start.2) | copy-done | bytes 1048600
  4.0 0.0 copy-start.3
  4.0 1.2 %copy-done.3 = f32[4,256,256]{2,1,0:T(8,128)S(1)} copy-done((f32[4,256,256]{2,1,0:T(8,128)S(1)}, f32[4,256,256]{2,1,0:T(8,128)}, u32[]{:S(2)}) %copy-start.3) | copy-done | bytes 1048600
  5.2 0.0 copy-start.1
  5.2 92.3 %shard_map.37 = (bf16[4096,1024]{1,0:T(8,128)(2,1)S(1)}, bf16[1024,768]{1,0:T(8,128)(2,1)S(1)}, f32[256,768]{1,0:T(8,128)S(1)}) custom-call(bf16[4096,768]{1,0:T(8,128)(2,1)S(1)} %copy-done, bf16[512,1024]{1,0:T(8,128)(2,1)S(1)} %copy-done.2, f32[4,256,256]{2,1,0:T(8,128)S(1)} %copy-done.3), custom_call_target="tpu_custom_call" | custom-call | tf_op jit(solution)/shard_map/pallas_call | solution.py:230
  97.6 0.0 copy-done.1
  97.6 9.6 %shard_map.38 = f32[4096,768]{1,0:T(8,128)} custom-call(s32[1]{0:T(128)} %bitcast.row_ref, bf16[4096,768]{1,0:T(8,128)(2,1)S(1)} %copy-done.1, bf16[4096,1024]{1,0:T(8,128)(2,1)S(1)} %get-tuple-element.8.gathered_ref, bf16[1024,768]{1,0:T(8,128)(2,1)S(1)} %get-tuple-element.9.shared_ref, f32[256,768]{1,0:T(8,128)S(1)} %get-tuple-element.10.solved_ref), custom_call_target="tpu_custom_call" | custom-call | tf_op jit(solution)/shard_map/pallas_call | solution.py:252
Async XLA Ops:
  0.0 2.8 %copy-start = (bf16[4096,768]{1,0:T(8,128)(2,1)S(1)}, bf16[4096,768]{1,0:T(8,128)(2,1)}, u32[]{:S(2)}) copy-start(bf16[4096,768]{1,0:T(8,128)(2,1)} %rhs_ref.3) | copy-start | bytes 18874372
  2.8 1.2 %copy-start.2 = (bf16[512,1024]{1,0:T(8,128)(2,1)S(1)}, bf16[512,1024]{1,0:T(8,128)(2,1)}, u32[]{:S(2)}) copy-start(bf16[512,1024]{1,0:T(8,128)(2,1)} %factor_ref.1) | copy-start | bytes 3145732
  4.0 1.2 %copy-start.3 = (f32[4,256,256]{2,1,0:T(8,128)S(1)}, f32[4,256,256]{2,1,0:T(8,128)}, u32[]{:S(2)}) copy-start(f32[4,256,256]{2,1,0:T(8,128)} %inverse_ref.1) | copy-start | bytes 3145732
  5.2 92.3 %copy-start.1 = (bf16[4096,768]{1,0:T(8,128)(2,1)S(1)}, bf16[4096,768]{1,0:T(8,128)(2,1)}, u32[]{:S(2)}) copy-start(bf16[4096,768]{1,0:T(8,128)(2,1)} %rhs_ref.3) | copy-start | bytes 18874372

commit v2 on v1

--- a/solution.py
+++ b/solution.py
@@ -8,7 +8,7 @@
 from jax.sharding import PartitionSpec as P
 
 MESH = pl.DeviceIdType.MESH
-UP, DOWN, RIGHT, LEFT = range(4)
+UP, DOWN, RIGHT, LEFT = 0, 1, 2, 3
 
 
 def every(*conditions):
@@ -27,9 +27,9 @@
 
 def gather_and_solve(
     rows, layers, lanes, parts,
-    rhs_ref, factor_ref, inverse_ref,
-    gathered, shared, own_solved,
-    lead, panel_rows,
+    rhs_ref, factor_ref, inverse_hbm,
+    gathered, shared, own_solved, partial,
+    inverse_ref, lead, panel_rows, factor_held, rhs_held,
     send_sem, recv_sem, lead_send, lead_recv, panel_send, panel_recv, local_sem,
 ):
     panels, width, _ = inverse_ref.shape
@@ -106,6 +106,8 @@
     own_lead = pltpu.make_async_copy(rhs_ref.at[pl.ds(0, width)], lead.at[lax.rem(row, panels)], local_sem.at[1])
     run_if(owner, own_lead.start)
     run_if(owner, own_lead.wait)
+    fetch_inverse = pltpu.make_async_copy(inverse_hbm, inverse_ref, local_sem.at[3])
+    fetch_inverse.start()
     own_block.wait()
 
     def exchange_panel(q):
@@ -114,22 +116,23 @@
                 run_if(row == k, lambda k=k, off=off: send_panel(k, off, q).start())
                 pending.append((row == k, lambda k=k, off=off: send_panel(k, off, q).wait_send()))
 
+    turn = 1 - 2 * (z // (layers // 2))
+
     def pass_on(q):
         for d in range(1, layers):
-            below, above = z >= d, z + d < layers
-            source = col - d * lanes
-            arrive(below, source, q)
-            send(every(below, can[UP]), UP, col + lanes, source, q)
-            kept = z % 2 == 0 if balanced and d == 1 and q >= half else True
-            for way in (RIGHT, LEFT):
-                send(every(below, can[way], kept), way, col + shift[way], source, q)
-            source_above = col + d * lanes
-            arrive(above, source_above, q)
-            send(every(above, can[DOWN]), DOWN, col - lanes, source_above, q)
-            kept = z % 2 == 1 if balanced and d == 1 and q >= half else True
-            for way in (RIGHT, LEFT):
-                send(every(above, can[way], kept), way, col + shift[way], source_above, q)
-
+            for side in (turn, -turn):
+                layer = z + side * d
+                onward = z - side
+                inside = jnp.logical_and(layer >= 0, layer < layers)
+                source = layer * lanes + y
+                arrive(inside, source, q)
+                go_on = jnp.logical_and(onward >= 0, onward < layers)
+                send(every(inside, go_on), (side + 1) // 2, onward * lanes + y, source, q)
+                kept = layer != partner if balanced and d == 1 and q >= half else True
+                for way in (RIGHT, LEFT):
+                    send(every(inside, can[way], kept), way, col + shift[way], source, q)
+
+    partner = z + 1 - 2 * (z % 2)
     other = z * lanes + (lanes - 1 - y)
     for q in range(parts):
         if q + 2 < parts:
@@ -139,10 +142,11 @@
             if 1 <= q <= panel_parts:
                 arrive(y == 1, 0, q - 1)
                 exchange_panel(q - 1)
-            if q >= half:
-                arrive(True, other, q)
-                send(True, z % 2, col + lanes * (1 - 2 * (z % 2)), other, q)
-    if not balanced:
+    if balanced:
+        for q in range(half, parts):
+            arrive(True, other, q)
+            send(True, z % 2, col + lanes * (1 - 2 * (z % 2)), other, q)
+    else:
         for q in range(parts):
             for s in range(1, lanes):
                 for layer in range(layers):
@@ -173,6 +177,7 @@
             ).wait_recv()
         run_if(row != k, other_lead)
 
+    fetch_inverse.wait()
     tile = min(256, shared.shape[1])
 
     @pl.loop(0, shared.shape[1] // tile)
@@ -193,6 +198,34 @@
                 own_solved[:, at] = solved
             run_if(row == k, keep)
 
+    def fetch(layer, slot):
+        at = pl.ds(pl.multiple_of((layer * lanes + y) * depth, depth), depth)
+        return (
+            pltpu.make_async_copy(gathered.at[at], factor_held.at[slot], local_sem.at[4 + slot]),
+            pltpu.make_async_copy(rhs_ref.at[at], rhs_held.at[slot], local_sem.at[6 + slot]),
+        )
+
+    for copy in fetch(0, 0):
+        copy.start()
+
+    @pl.loop(0, layers)
+    def _(layer):
+        slot = lax.rem(layer, 2)
+
+        @pl.when(layer + 1 < layers)
+        def _():
+            for copy in fetch(layer + 1, 1 - slot):
+                copy.start()
+
+        for copy in fetch(layer, slot):
+            copy.wait()
+        update = jnp.dot(factor_held[slot], shared[...], preferred_element_type=jnp.float32)
+        partial[pl.ds(pl.multiple_of(layer * depth, depth), depth), :] = rhs_held[slot].astype(jnp.float32) - update
+
+    def keep_solved():
+        partial[:width] = own_solved[...]
+    run_if(jnp.logical_and(owner, y == 0), keep_solved)
+
     if balanced:
         for layer in range(layers):
             for q in range(parts):
@@ -207,15 +240,51 @@
         run_if(condition, finish)
 
 
-def multiply(row_ref, rhs_ref, gathered_ref, shared_ref, solved_ref, out_ref):
-    step = pl.program_id(0)
+def multiply(panels, layers, lanes, rhs_ref, gathered_ref, shared_ref, solved_ref, partial_ref, out_ref, held, sem, part_sem):
     width = solved_ref.shape[0]
-    update = jnp.dot(gathered_ref[...], shared_ref[...], preferred_element_type=jnp.float32)
-    out_ref[...] = rhs_ref[...].astype(jnp.float32) - update
-
-    @pl.when(jnp.logical_and(step == 0, row_ref[0] == 1))
-    def _():
-        out_ref[:width] = solved_ref[...]
+    depth = held.shape[1]
+    owner = lax.axis_index("row") < panels
+    y = lax.axis_index("col") % lanes
+    others = lanes - 1
+    steps = layers * others
+
+    def hand_on(layer):
+        at = pl.ds(pl.multiple_of((layer * lanes + y) * depth, depth), depth)
+        return pltpu.make_async_copy(partial_ref.at[pl.ds(layer * depth, depth)], out_ref.at[at], part_sem.at[layer])
+
+    def source_of(step):
+        return (step // others) * lanes + lax.rem(y + 1 + lax.rem(step, others), lanes)
+
+    def write(step, slot):
+        at = pl.ds(pl.multiple_of(source_of(step) * depth, depth), depth)
+        return pltpu.make_async_copy(held.at[slot], out_ref.at[at], sem.at[slot])
+
+    for layer in range(layers):
+        hand_on(layer).start()
+
+    @pl.loop(0, steps)
+    def _(step):
+        slot = lax.rem(step, 2)
+
+        @pl.when(step >= 2)
+        def _():
+            write(step - 2, slot).wait()
+
+        source = source_of(step)
+        at = pl.ds(pl.multiple_of(source * depth, depth), depth)
+        update = jnp.dot(gathered_ref[at, :], shared_ref[...], preferred_element_type=jnp.float32)
+        held[slot] = rhs_ref[at, :].astype(jnp.float32) - update
+
+        @pl.when(jnp.logical_and(source == 0, owner))
+        def _():
+            held[slot, :width] = solved_ref[...]
+
+        write(step, slot).start()
+
+    for step in range(max(steps - 2, 0), steps):
+        write(step, step % 2).wait()
+    for layer in range(layers):
+        hand_on(layer).wait()
 
 
 def per_device(rows, layers, lanes, right_sides, factor_panels, inverse_blocks):
@@ -227,44 +296,38 @@
     dma = pltpu.SemaphoreType.DMA
     anywhere = pl.BlockSpec(memory_space=pl.ANY)
     in_vmem = pl.BlockSpec(memory_space=pltpu.VMEM)
-    gathered, shared, own_solved = pl.pallas_call(
+    gathered, shared, own_solved, partial = pl.pallas_call(
         functools.partial(gather_and_solve, rows, layers, lanes, parts),
         out_shape=(
             jax.ShapeDtypeStruct((cols * depth, across), factor_panels.dtype),
             jax.ShapeDtypeStruct((panels * width, count), jnp.bfloat16),
             jax.ShapeDtypeStruct((width, count), jnp.float32),
+            jax.ShapeDtypeStruct((layers * depth, count), jnp.float32),
         ),
-        in_specs=[anywhere, anywhere, in_vmem],
-        out_specs=(anywhere, in_vmem, in_vmem),
+        in_specs=[anywhere, anywhere, anywhere],
+        out_specs=(anywhere, in_vmem, in_vmem, in_vmem),
         scratch_shapes=[
+            pltpu.VMEM(inverse_blocks.shape, inverse_blocks.dtype),
             pltpu.VMEM((panels, width, count), right_sides.dtype),
             pltpu.VMEM((panels - 1, width, (panels - 1) * width), factor_panels.dtype),
+            pltpu.VMEM((2, depth, across), factor_panels.dtype),
+            pltpu.VMEM((2, depth, count), right_sides.dtype),
             dma((4, cols, parts)), dma((cols, parts)),
-            dma((rows,)), dma((panels,)), dma((rows, parts)), dma((panels, parts)), dma((3,)),
+            dma((rows,)), dma((panels,)), dma((rows, parts)), dma((panels, parts)), dma((8,)),
         ],
         compiler_params=pltpu.CompilerParams(
-            collective_id=0, has_side_effects=True, vmem_limit_bytes=24 << 20
+            collective_id=0, has_side_effects=True, vmem_limit_bytes=16 << 20
         ),
     )(right_sides, factor_panels, inverse_blocks)
 
-    tile = 512
-    is_owner = (lax.axis_index("row") < panels).astype(jnp.int32).reshape(1)
     return pl.pallas_call(
-        multiply,
+        functools.partial(multiply, panels, layers, lanes),
         out_shape=jax.ShapeDtypeStruct((height, count), jnp.float32),
-        grid_spec=pltpu.PrefetchScalarGridSpec(
-            num_scalar_prefetch=1,
-            grid=(height // tile,),
-            in_specs=[
-                pl.BlockSpec((tile, count), lambda i, s: (i, 0)),
-                pl.BlockSpec((tile, across), lambda i, s: (i, 0)),
-                pl.BlockSpec((across, count), lambda i, s: (0, 0)),
-                pl.BlockSpec((width, count), lambda i, s: (0, 0)),
-            ],
-            out_specs=pl.BlockSpec((tile, count), lambda i, s: (i, 0)),
-        ),
-        compiler_params=pltpu.CompilerParams(vmem_limit_bytes=32 << 20),
-    )(is_owner, right_sides, gathered, shared, own_solved)
+        in_specs=[in_vmem] * 5,
+        out_specs=anywhere,
+        scratch_shapes=[pltpu.VMEM((2, depth, count), jnp.float32), dma((2,)), dma((layers,))],
+        compiler_params=pltpu.CompilerParams(vmem_limit_bytes=16 << 20),
+    )(right_sides, gathered, shared, own_solved, partial)
 
 
 def solution(mesh):

time: 107 us -> 103 us (0.963)
  Pallas kernels: 102 us -> 97.7 us
    pallas_call x1, Pallas kernels: 9.58 us -> 6.35 us  [per_device(): pl.pallas_call(functools.partial(multiply, panels, layers, lanes), out_sh...]
    unnamed x8 -> x6, local copies, waits for them, and re-layouts: 5.24 us -> 5.23 us
where the time goes in v2:
time: 103 us
  Pallas kernels  97.7 us (95%)
  local copies, waits for them, and re-layouts  5.23 us (5%)
    pallas_call x1, Pallas kernels, per_device(): pl.pallas_call(functools.partial(gather_and_solve, rows, layers, lanes, p...  91.3 us
    pallas_call x1, Pallas kernels, per_device(): pl.pallas_call(functools.partial(multiply, panels, layers, lanes), out_sh...  6.35 us
    unnamed x6, local copies, waits for them, and re-layouts  5.23 us

profile of v2, /device:TPU:0, one launch (start us, length us, event | category | flops | bytes accessed | tf_op | source)
XLA Modules:
  0.0 102.9 jit_solution(11059996003423625760)
XLA Ops:
  0.0 0.0 copy-start
  0.0 2.8 %copy-done = bf16[4096,768]{1,0:T(8,128)(2,1)S(1)} copy-done((bf16[4096,768]{1,0:T(8,128)(2,1)S(1)}, bf16[4096,768]{1,0:T(8,128)(2,1)}, u32[]{:S(2)}) %copy-start) | copy-done | bytes 6291480
  2.8 0.0 copy-start.1
  2.8 1.2 %copy-done.1 = bf16[512,1024]{1,0:T(8,128)(2,1)S(1)} copy-done((bf16[512,1024]{1,0:T(8,128)(2,1)S(1)}, bf16[512,1024]{1,0:T(8,128)(2,1)}, u32[]{:S(2)}) %copy-start.1) | copy-done | bytes 1048600
  4.0 0.0 copy-start.2
  4.0 1.2 %copy-done.2 = f32[4,256,256]{2,1,0:T(8,128)S(1)} copy-done((f32[4,256,256]{2,1,0:T(8,128)S(1)}, f32[4,256,256]{2,1,0:T(8,128)}, u32[]{:S(2)}) %copy-start.2) | copy-done | bytes 1048600
  5.2 91.3 %shard_map.37 = (bf16[4096,1024]{1,0:T(8,128)(2,1)S(1)}, bf16[1024,768]{1,0:T(8,128)(2,1)S(1)}, f32[256,768]{1,0:T(8,128)S(1)}, f32[2048,768]{1,0:T(8,128)S(1)}) custom-call(bf16[4096,768]{1,0:T(8,128)(2,1)S(1)} %copy-done, bf16[512,1024]{1,0:T(8,128)(2,1)S(1)} %copy-done.1, f32[4,256,256]{2,1,0:T(8,128)S(1)} %copy-done.2), custom_call_target="tpu_custom_call" | custom-call | tf_op jit(solution)/shard_map/pallas_call | solution.py:299
  96.5 6.4 %shard_map.38 = f32[4096,768]{1,0:T(8,128)} custom-call(bf16[4096,768]{1,0:T(8,128)(2,1)S(1)} %copy-done, bf16[4096,1024]{1,0:T(8,128)(2,1)S(1)} %get-tuple-element.9.gathered_ref, bf16[1024,768]{1,0:T(8,128)(2,1)S(1)} %get-tuple-element.10.shared_ref, f32[256,768]{1,0:T(8,128)S(1)} %get-tuple-element.11.solved_ref, ...), custom_call_target="tpu_custom_call" | custom-call | tf_op jit(solution)/shard_map/pallas_call | solution.py:323
Async XLA Ops:
  0.0 2.8 %copy-start = (bf16[4096,768]{1,0:T(8,128)(2,1)S(1)}, bf16[4096,768]{1,0:T(8,128)(2,1)}, u32[]{:S(2)}) copy-start(bf16[4096,768]{1,0:T(8,128)(2,1)} %rhs_ref.3) | copy-start | bytes 18874372
  2.8 1.2 %copy-start.1 = (bf16[512,1024]{1,0:T(8,128)(2,1)S(1)}, bf16[512,1024]{1,0:T(8,128)(2,1)}, u32[]{:S(2)}) copy-start(bf16[512,1024]{1,0:T(8,128)(2,1)} %factor_ref.1) | copy-start | bytes 3145732
  4.0 1.2 %copy-start.2 = (f32[4,256,256]{2,1,0:T(8,128)S(1)}, f32[4,256,256]{2,1,0:T(8,128)}, u32[]{:S(2)}) copy-start(f32[4,256,256]{2,1,0:T(8,128)} %inverse_hbm.1) | copy-start | bytes 3145732
